TPU v7x, 32 devices: a whole 2x2x4 slice. The times are simulated.
32 devices in a mesh: dp: 8 (over z, y), expert: 4 (over x, core).
Axes of the slice: x: 2, y: 2, z: 4, core: 2. Of those that a mesh axis runs over, the one named last changes fastest.
Arguments:
- residual: bfloat16 [512, 4096], P(('dp', 'expert')), may hold values from -8.2 to 8.2
- queries: bfloat16 [512, 4096], P('dp', 'expert'), may hold values from -24 to 24
- new_keys: bfloat16 [512, 1024], P('dp', 'expert'), may hold values from -6 to 6
- new_values: bfloat16 [512, 1024], P('dp', 'expert'), may hold values from -6 to 6
- cache_keys: bfloat16 [16, 1024, 1024], P('dp', None, 'expert'), may hold values from -8 to 8
- cache_values: bfloat16 [16, 1024, 1024], P('dp', None, 'expert'), may hold values from -6 to 6
- out_weight: bfloat16 [4096, 4096], P('expert', 'dp'), may hold values from -1 to 1
- ffn_gain: float32 [4096], replicated, may hold values from 0.1 to 1.9
- router: bfloat16 [4096, 8], replicated, may hold values from -0.0234375 to 0.0234375
- routes: int32 [512, 2], P(('dp', 'expert')), may hold values from 0 to 7, all different within a row; in each aligned block of 64 rows (0 to 63, 64 to 127, ...) at most 24 rows name the same one
- w_gate: bfloat16 [8, 4096, 14336], P('expert', None, 'dp'), may hold values from -0.09375 to 0.09375
- w_up: bfloat16 [8, 4096, 14336], P('expert', None, 'dp'), may hold values from -0.09375 to 0.09375
- w_down: bfloat16 [8, 14336, 4096], P('expert', 'dp'), may hold values from -0.046875 to 0.046875
- summary_gain: float32 [4096], P('expert'), may hold values from 0.1 to 1.9
- reduce_scale: float32 [32], P('expert'), may hold values from 0.1 to 30
- assign: int32 [16], replicated, may hold values from 0 to 3
Outputs:
- summary: bfloat16 [16, 4096], P('dp', 'expert')
- reduced: bfloat16 [16, 4096], P('dp', 'expert')
Inputs may be any that keep to these rules, and one draw needn't show every extreme that they name: `routes`: each token names 2 different experts and every expert is named by some token; among the tokens of one dp index (aligned blocks of 64 rows) no expert is named by more than 24 tokens, and that bound is reached in some block.
All inputs are finite; a program needn't handle non-finite values.
Results may differ from a plain program's by a relative error of at most 0.017.
Values may be sent and summed in bfloat16 or wider, within the bound.
A program may use at most 192 MiB of HBM per device.

v0:
```python
import math

import jax
import jax.numpy as jnp
from jax import lax
from jax.sharding import PartitionSpec as P

HEADS = 32
KVH = 8
HD = 128
EXPERTS = 8
WIN = 32
GROUP_CAP = 24


EPSILON = 1e-05


def attend(queries, new_keys, new_values, cache_keys, cache_values):
    span_count, cache_len, kv_width = cache_keys.shape
    kv_local = kv_width // HD
    group = HEADS // KVH
    window = queries.shape[0] // span_count
    query_view = queries.reshape(span_count, window, kv_local, group, HD)
    fresh_keys = new_keys.reshape(span_count, window, kv_local, HD)
    fresh_values = new_values.reshape(span_count, window, kv_local, HD)
    stored_keys = cache_keys.reshape(span_count, cache_len, kv_local, HD)
    stored_values = cache_values.reshape(span_count, cache_len, kv_local, HD)
    factor = 1.0 / math.sqrt(HD)
    past_scores = (
        jnp.einsum("ctkgd,cpkd->ckgtp", query_view, stored_keys, preferred_element_type=jnp.float32)
        * factor
    )
    fresh_scores = (
        jnp.einsum("ctkgd,cskd->ckgts", query_view, fresh_keys, preferred_element_type=jnp.float32)
        * factor
    )
    causal = jnp.arange(window)[:, None] >= jnp.arange(window)[None, :]
    fresh_scores = jnp.where(causal, fresh_scores, -jnp.inf)
    highest = jnp.maximum(jnp.max(past_scores, axis=-1), jnp.max(fresh_scores, axis=-1))[..., None]
    past_exp = jnp.exp(past_scores - highest)
    fresh_exp = jnp.exp(fresh_scores - highest)
    totals = jnp.sum(past_exp, axis=-1, keepdims=True) + jnp.sum(fresh_exp, axis=-1, keepdims=True)
    past_weights = (past_exp / totals).astype(jnp.bfloat16)
    fresh_weights = (fresh_exp / totals).astype(jnp.bfloat16)
    context = jnp.einsum(
        "ckgtp,cpkd->ctkgd", past_weights, stored_values, preferred_element_type=jnp.float32
    )
    context = context + jnp.einsum(
        "ckgts,cskd->ctkgd", fresh_weights, fresh_values, preferred_element_type=jnp.float32
    )
    return context.astype(jnp.bfloat16).reshape(span_count * window, kv_local * group * HD)


def expert_rows(rows, w_gate, w_up, w_down):
    gate_proj = jnp.einsum("ned,edf->nef", rows, w_gate, preferred_element_type=jnp.float32)
    up_proj = jnp.einsum("ned,edf->nef", rows, w_up, preferred_element_type=jnp.float32)
    hidden = (jax.nn.silu(gate_proj) * up_proj).astype(jnp.bfloat16)
    return jnp.einsum("nef,efd->ned", hidden, w_down, preferred_element_type=jnp.float32)


def shards(
    residual,
    queries,
    new_keys,
    new_values,
    cache_keys,
    cache_values,
    out_weight,
    ffn_gain,
    router,
    routes,
    w_gate,
    w_up,
    w_down,
    summary_gain,
    reduce_scale,
    assign,
):
    expert_count = lax.axis_size("expert")
    dp_index = lax.axis_index("dp")
    column = lax.axis_index("expert")
    span_local = cache_keys.shape[0]
    tok_local = residual.shape[0]
    width = residual.shape[1]
    slice_width = width // expert_count
    highest_precision = lax.Precision.HIGHEST
    attended = attend(queries, new_keys, new_values, cache_keys, cache_values)
    head_terms = jnp.dot(
        attended,
        lax.all_gather(out_weight, "dp", axis=1, tiled=True),
        preferred_element_type=jnp.float32,
    )
    mixed = residual.astype(jnp.float32) + lax.psum_scatter(
        head_terms, "expert", scatter_dimension=0, tiled=True
    )
    normed = (
        mixed * lax.rsqrt(jnp.mean(mixed * mixed, axis=-1, keepdims=True) + EPSILON) * ffn_gain
    ).astype(jnp.bfloat16)
    logits = jnp.dot(normed, router, preferred_element_type=jnp.float32)
    expert_ids = jnp.arange(EXPERTS, dtype=jnp.int32)
    first = routes[:, 0:1] == expert_ids[None, :]
    second = routes[:, 1:2] == expert_ids[None, :]
    first_logit = jnp.sum(jnp.where(first, logits, 0.0), axis=-1)
    second_logit = jnp.sum(jnp.where(second, logits, 0.0), axis=-1)
    partner = jnp.where(first, routes[:, 1:2], jnp.where(second, routes[:, 0:1], -1))
    outgoing = jnp.where((partner >= 0).T[:, :, None], normed[None, :, :], 0)
    arrived_rows, arrived_partner = (
        lax.all_to_all(outgoing, "expert", split_axis=0, concat_axis=1, tiled=True),
        lax.all_to_all(partner.T, "expert", split_axis=0, concat_axis=1, tiled=True),
    )
    present = (arrived_partner >= 0).astype(jnp.int32)
    position = jnp.cumsum(present, axis=1) - 1
    picker = (present[:, None, :] > 0) & (
        position[:, None, :] == jnp.arange(GROUP_CAP)[None, :, None]
    )
    compact = jnp.einsum(
        "eks,esd->ked",
        picker.astype(jnp.bfloat16),
        arrived_rows,
        preferred_element_type=jnp.float32,
    ).astype(jnp.bfloat16)
    token_span = (column * tok_local + jnp.arange(tok_local)) // WIN
    pool_matrix = (token_span[None, :] == jnp.arange(span_local)[:, None]).astype(jnp.float32)
    gathered = lax.all_gather(compact, "dp", axis=0, tiled=True)
    returned = lax.psum_scatter(
        expert_rows(gathered, w_gate, w_up, w_down), "dp", scatter_dimension=0, tiled=True
    )
    spread = jnp.einsum(
        "eks,ked->esd", picker.astype(jnp.float32), returned, precision=highest_precision
    )
    back = lax.all_to_all(spread, "expert", split_axis=1, concat_axis=0, tiled=True)
    gate_table = jnp.where(first, jax.nn.sigmoid(first_logit - second_logit)[:, None], 0.0)
    gate_table = gate_table + jnp.where(
        second, jax.nn.sigmoid(second_logit - first_logit)[:, None], 0.0
    )
    token_out = mixed + jnp.einsum("te,etd->td", gate_table, back, precision=highest_precision)
    pooled_local = jnp.dot(pool_matrix, token_out, precision=highest_precision)
    pooled = lax.psum_scatter(pooled_local, "expert", scatter_dimension=1, tiled=True)
    squares = lax.psum(jnp.sum(pooled * pooled, axis=-1), "expert")
    summary = (pooled * lax.rsqrt(squares / width + EPSILON)[:, None] * summary_gain).astype(
        jnp.bfloat16
    )
    everyone = lax.all_gather(summary, "dp", axis=0, tiled=True)
    heads_local = slice_width // HD
    mine = summary.reshape(span_local, heads_local, HD)
    others = everyone.reshape(everyone.shape[0], heads_local, HD)
    factor = reduce_scale / math.sqrt(HD)
    scores = (
        jnp.einsum("chd,khd->hck", mine, others, preferred_element_type=jnp.float32)
        * factor[:, None, None]
    )
    own_assign = lax.dynamic_slice_in_dim(assign, dp_index * span_local, span_local)
    same = own_assign[:, None] == assign[None, :]
    scores = jnp.where(same[None], scores, -jnp.inf)
    highest = jnp.max(scores, axis=-1, keepdims=True)
    expo = jnp.exp(scores - highest)
    weights = (expo / jnp.sum(expo, axis=-1, keepdims=True)).astype(jnp.bfloat16)
    reduced = jnp.einsum("hck,khd->chd", weights, others, preferred_element_type=jnp.float32)
    reduced = reduced.reshape(span_local, slice_width).astype(jnp.bfloat16)
    return (summary, reduced)


def solution(mesh):
    return jax.shard_map(
        shards,
        mesh=mesh,
        in_specs=(
            P(("dp", "expert"), None),
            P("dp", "expert"),
            P("dp", "expert"),
            P("dp", "expert"),
            P("dp", None, "expert"),
            P("dp", None, "expert"),
            P("expert", "dp"),
            P(),
            P(),
            P(("dp", "expert"), None),
            P("expert", None, "dp"),
            P("expert", None, "dp"),
            P("expert", "dp", None),
            P("expert"),
            P("expert"),
            P(),
        ),
        out_specs=(P("dp", "expert"), P("dp", "expert")),
        check_vma=False,
    )
```

profile of v0, /device:TPU:0, one launch (start us, length us, event | category | flops | bytes accessed | tf_op | source)
XLA Modules:
  0.0 525.4 jit_solution(7913883085659773262)
XLA Ops:
  7.2 0.0 copy-start
  7.2 0.0 all-gather.4.cloned.1.call-start
  7.3 0.7 all-gather.4.cloned.1.call-update
  7.9 0.0 reduce-scatter.6.cloned.1.call-start
  8.0 1.0 reshape.245
  9.0 1.3 reshape.244
  10.4 0.3 reshape.247
  10.7 0.3 fusion.43
  11.0 0.5 bitcast_reduce_fusion
  11.6 0.1 fusion.19
  11.6 0.5 fusion.5
  12.2 0.8 fusion.14
  13.0 0.3 fusion.9
  13.2 0.1 copy.60
  13.3 0.1 reshape.249
  13.4 0.0 copy-start.10
  13.4 0.0 copy-start.3
  13.4 124.8 %all-gather.4.cloned.1.call-done = bf16[1024,4096]{1,0:T(8,128)(2,1)} async-done(((bf16[1024,512]{1,0:T(8,128)(2,1)}), bf16[1024,4096]{1,0:T(8,128)(2,1)}) %all-gather.4.cloned.1.call-update) | async-done | bytes 8388624 | tf_op jit(solution)/shard_map/all_gather | solution.py:91
  138.2 6.0 %fusion.49 = f32[64,4096]{1,0:T(8,128)} fusion(bf16[64,1024]{1,0:T(8,128)(2,1)S(1)} %reshape.249, bf16[1024,4096]{1,0:T(8,128)(2,1)} %all-gather.4.cloned.1.call-done), kind=kOutput, calls=%fused_computation.94 | convolution fusion | flops 536870912 | bytes 9568256 | tf_op jit(solution)/shard_map/dot_general | solution.py:89
  144.2 0.0 reduce-scatter.6.cloned.1.call-update
  144.3 0.7 compare_select_fusion.1
  145.0 3.2 all-to-all-start
  148.2 19.3 %reduce-scatter.6.cloned.1.call-done = f32[16,4096]{1,0:T(8,128)} async-done(((f32[64,4096]{1,0:T(8,128)}), f32[16,4096]{1,0:T(8,128)}) %reduce-scatter.6.cloned.1.call-update) | async-done | bytes 262160 | tf_op jit(solution)/shard_map/reduce_scatter | solution.py:94
  167.5 1.1 multiply_reduce_fusion
  168.6 1.0 multiply_convert_fusion.1
  169.7 1.1 broadcast_select_fusion
  170.8 3.5 all-to-all-start.1
  174.3 0.0 all-gather.6.cloned.1.call-start
  174.4 0.1 reshape.252
  174.5 0.2 reduce_window_sum.11
  174.7 14.0 %all-to-all-done.1 = bf16[8,16,4096]{2,1,0:T(8,128)(2,1)S(1)} async-done(((bf16[8,16,4096]{2,1,0:T(8,128)(2,1)}), bf16[8,16,4096]{2,1,0:T(8,128)(2,1)S(1)}, u32[]{:S(2)}, u32[]{:S(2)}) %all-to-all-start.1) | async-done | bytes 1048608 | tf_op jit(solution)/shard_map/all_to_all | solution.py:109
  188.7 0.1 copy.62
  188.8 1.0 fusion.1
  189.9 0.0 all-gather.6.cloned.1.call-update
  189.9 0.2 reduce-scatter.8.cloned.1.call-start
  190.1 60.4 %all-gather.6.cloned.1.call-done = bf16[192,2,4096]{2,0,1:T(8,128)(2,1)} async-done(((bf16[24,2,4096]{2,0,1:T(8,128)(2,1)}), bf16[192,2,4096]{2,0,1:T(8,128)(2,1)}) %all-gather.6.cloned.1.call-update) | async-done | bytes 3145744 | tf_op jit(solution)/shard_map/all_gather | solution.py:125
  250.5 13.9 %convolution_bitcast_fusion.3 = f32[192,2,1792]{2,0,1:T(8,128)S(1)} fusion(bf16[192,2,4096]{2,0,1:T(8,128)(2,1)} %all-gather.6.cloned.1.call-done, bf16[2,4096,1792]{2,1,0:T(8,128)(2,1)} %param.26), kind=kOutput, calls=%fused_computation.6 | convolution fusion | flops 5637144576 | bytes 35258368 | tf_op jit(solution)/shard_map/ned,edf->nef/dot_general | solution.py:56
  264.4 12.5 %multiply_convert_fusion = bf16[192,2,1792]{2,0,1:T(8,128)(2,1)S(1)} fusion(f32[192,2,1792]{2,0,1:T(8,128)S(1)} %convolution_bitcast_fusion.3, bf16[192,2,4096]{2,0,1:T(8,128)(2,1)S(1)} %copy-done.1, bf16[2,4096,1792]{2,1,0:T(8,128)(2,1)} %param.27), kind=kOutput, calls=%fused_computation.7 | convolution fusion | flops 5641273344 | bytes 36634624 | tf_op jit(solution)/shard_map/ned,edf->nef/dot_general | solution.py:57
  276.9 14.2 %convolution_bitcast_fusion = f32[192,2,4096]{2,0,1:T(8,128)} fusion(bf16[192,2,1792]{2,0,1:T(8,128)(2,1)S(1)} %multiply_convert_fusion, bf16[2,1792,4096]{2,1,0:T(8,128)(2,1)} %param.28), kind=kOutput, calls=%fused_computation.1 | convolution fusion | flops 5637144576 | bytes 37027840 | tf_op jit(solution)/shard_map/nef,efd->ned/dot_general | solution.py:59
  291.2 0.0 reduce-scatter.8.cloned.1.call-update
  291.2 116.7 %reduce-scatter.8.cloned.1.call-done = f32[24,2,4096]{2,0,1:T(8,128)} async-done(((f32[192,2,4096]{2,0,1:T(8,128)}), f32[24,2,4096]{2,0,1:T(8,128)}) %reduce-scatter.8.cloned.1.call-update) | async-done | bytes 786448 | tf_op jit(solution)/shard_map/reduce_scatter | solution.py:126
  407.9 2.2 fusion.29
  410.1 3.0 copy.63
  413.0 3.7 all-to-all-start.2
  416.8 0.3 reduce-scatter.10.cloned.1.call-start
  417.1 0.1 dynamic_slice.3
  417.2 0.2 select_reduce_fusion.1
  417.4 0.1 copy.74
  417.4 25.0 %all-to-all-done.2 = f32[2,64,4096]{2,0,1:T(2,128)S(1)} async-done(((f32[2,64,4096]{2,0,1:T(2,128)}), f32[2,64,4096]{2,0,1:T(2,128)S(1)}, u32[]{:S(2)}, u32[]{:S(2)}) %all-to-all-start.2) | async-done | bytes 2097184 | tf_op jit(solution)/shard_map/all_to_all | solution.py:132
  442.4 1.2 copy.64
  443.7 0.2 copy.65
  443.9 2.9 fusion.3
  446.8 3.2 convolution_bitcast_fusion.1
  449.9 0.0 reduce-scatter.10.cloned.1.call-update
  450.0 0.1 broadcast_compare_fusion
  450.0 29.7 %reduce-scatter.10.cloned.1.call-done = f32[1024,2]{1,0:T(8,128)} async-done(((f32[4096,2]{1,0:T(8,128)}), f32[1024,2]{1,0:T(8,128)}) %reduce-scatter.10.cloned.1.call-update) | async-done | bytes 8208
  479.8 1.2 copy.86
  481.0 0.1 multiply_reduce_fusion.1
  481.1 5.8 %psum.7 = f32[2]{0:T(128)S(1)} all-reduce(f32[2]{0:T(128)S(1)} %multiply_reduce_fusion.1), channel_id=1, replica_groups=mesh['dp'=8,'expert'=4] {'expert'}, use_global_device_ids=true, to_apply=%region_12.13 | all-reduce | flops 2 | bytes 16 | tf_op jit(solution)/shard_map/psum | solution.py:140
  486.9 0.1 fusion.63
  487.0 0.1 multiply_convert_fusion.2
  487.1 30.6 %all-gather = bf16[8,2,1024]{2,1,0:T(2,128)(2,1)S(1)} all-gather(bf16[1,2,1024]{2,1,0:T(2,128)(2,1)S(1)} %fusion.63), channel_id=1, replica_groups=mesh['dp'=8,'expert'=4] {'dp'}, dimensions={0}, use_global_device_ids=true | all-gather | bytes 36864 | tf_op jit(solution)/shard_map/all_gather | solution.py:144
  517.7 0.3 fusion.44
  518.0 0.8 fusion.13
  (43 shorter events, 0.2 us)
Async XLA Ops:
  7.2 410.0 %copy-start = (bf16[4096,8]{0,1:T(8,128)(2,1)S(1)}, bf16[4096,8]{0,1:T(8,128)(2,1)}, u32[]{:S(2)}) copy-start(bf16[4096,8]{0,1:T(8,128)(2,1)} %param.24) | copy-start | bytes 196612
  7.2 3.1 copy-start.5
  7.2 3.2 copy-start.4
  7.2 3.5 copy-start.6
  7.2 131.0 %all-gather.4.cloned.1.call-start = ((), (), s32[]{:S(2)}) async-start(), calls=%async_computation.6 | async-start | bytes 9437184 | tf_op jit(solution)/shard_map/all_gather | solution.py:91
  7.9 159.5 %reduce-scatter.6.cloned.1.call-start = ((), (), s32[]{:S(2)}) async-start(), calls=%async_computation.7 | async-start | bytes 1310720 | tf_op jit(solution)/shard_map/reduce_scatter | solution.py:94
  13.4 130.9 %copy-start.10 = (s32[16,2]{0,1:T(2,128)S(1)}, s32[16,2]{0,1:T(2,128)}, u32[]{:S(2)}) copy-start(s32[16,2]{0,1:T(2,128)} %param.25) | copy-start | bytes 388
  13.4 154.1 %copy-start.3 = (bf16[16,4096]{1,0:T(8,128)(2,1)S(1)}, bf16[16,4096]{1,0:T(8,128)(2,1)}, u32[]{:S(2)}) copy-start(bf16[16,4096]{1,0:T(8,128)(2,1)} %param.16) | copy-start | bytes 393220
  13.4 155.2 %copy-start.7 = (f32[4096]{0:T(1024)S(1)}, f32[4096]{0:T(1024)}, u32[]{:S(2)}) copy-start(f32[4096]{0:T(1024)} %param.23) | copy-start | bytes 49156
  145.0 25.8 %all-to-all-start = ((s32[4,2,16]{2,1,0:T(2,128)}), s32[4,2,16]{2,1,0:T(2,128)S(1)}, u32[]{:S(2)}, u32[]{:S(2)}) async-start(s32[4,2,16]{2,1,0:T(2,128)} %compare_select_fusion.1), calls=%async_computation.1 | async-start | bytes 8192 | tf_op jit(solution)/shard_map/all_to_all | solution.py:110
  170.8 18.0 %all-to-all-start.1 = ((bf16[8,16,4096]{2,1,0:T(8,128)(2,1)}), bf16[8,16,4096]{2,1,0:T(8,128)(2,1)S(1)}, u32[]{:S(2)}, u32[]{:S(2)}) async-start(bf16[8,16,4096]{2,1,0:T(8,128)(2,1)} %broadcast_select_fusion), calls=%async_computation.2 | async-start | bytes 2097152 | tf_op jit(solution)/shard_map/all_to_all | solution.py:109
  174.3 76.2 %all-gather.6.cloned.1.call-start = ((), (), s32[]{:S(2)}) async-start(), calls=%async_computation.8 | async-start | bytes 3538944 | tf_op jit(solution)/shard_map/all_gather | solution.py:125
  189.9 218.0 %reduce-scatter.8.cloned.1.call-start = ((), (), s32[]{:S(2)}) async-start(), calls=%async_computation.9 | async-start | bytes 7077888 | tf_op jit(solution)/shard_map/reduce_scatter | solution.py:126
  250.5 13.9 %copy-start.1 = (bf16[192,2,4096]{2,0,1:T(8,128)(2,1)S(1)}, bf16[192,2,4096]{2,0,1:T(8,128)(2,1)}, u32[]{:S(2)}) copy-start(bf16[192,2,4096]{2,0,1:T(8,128)(2,1)} %all-gather.6.cloned.1.call-done) | copy-start | bytes 9437188
  413.0 4.0 copy-start.11
  413.0 29.4 %all-to-all-start.2 = ((f32[2,64,4096]{2,0,1:T(2,128)}), f32[2,64,4096]{2,0,1:T(2,128)S(1)}, u32[]{:S(2)}, u32[]{:S(2)}) async-start(f32[2,64,4096]{2,0,1:T(2,128)} %copy.63), calls=%async_computation.4 | async-start | bytes 4194304 | tf_op jit(solution)/shard_map/all_to_all | solution.py:132
  416.8 63.0 %reduce-scatter.10.cloned.1.call-start = ((), (), s32[]{:S(2)}) async-start(), calls=%async_computation.10 | async-start | bytes 2621440
  443.7 3.1 copy-start.2
  446.7 34.4 %copy-start.12 = (f32[8]{0:T(128)S(1)}, f32[8]{0:T(128)}, u32[]{:S(2)}) copy-start(f32[8]{0:T(128)} %param.30) | copy-start | bytes 100
  446.8 40.2 %copy-start.8 = (f32[1024]{0:T(1024)S(1)}, f32[1024]{0:T(1024)}, u32[]{:S(2)}) copy-start(f32[1024]{0:T(1024)} %param.29) | copy-start | bytes 12292
  487.1 31.8 %copy-start.9 = (bf16[2,1024]{1,0:T(2,128)(2,1)}, bf16[2,1024]{1,0:T(2,128)(2,1)S(1)}, u32[]{:S(2)}) copy-start(bf16[2,1024]{1,0:T(2,128)(2,1)S(1)} %multiply_convert_fusion.2) | copy-start | bytes 12292
Sparse Core Ops, SparseCore 0:
  10.1 128.0 all-gather.3
  144.4 23.0 reduce-scatter.5
  190.0 60.4 all-gather.5
  291.3 116.5 reduce-scatter.7
  450.1 29.6 reduce-scatter.9
where the time goes:
time: 526 us; the launch traced here: 525 us
  waiting for transfers between devices  391 us (74%)
  matrix products  59 us (11%)
  blocking collectives  36.4 us (7%)
  between operations  14.2 us (3%)
  starting transfers between devices  11.1 us (2%)
  local copies, waits for them, and re-layouts  8.8 us (2%)
    all_gather x1, waiting for transfers between devices, shards(): lax.all_gather(out_weight, 'dp', axis=1, tiled=True)  125 us
    reduce_scatter x1, waiting for transfers between devices, shards(): lax.psum_scatter(expert_rows(gathered, w_gate, w_up, w_down), 'dp', scatt...  117 us
    all_gather x1, waiting for transfers between devices, shards(): gathered = lax.all_gather(compact, 'dp', axis=0, tiled=True)  60.4 us
    all_gather x1, blocking collectives, shards(): everyone = lax.all_gather(summary, 'dp', axis=0, tiled=True)  30.6 us
    unnamed x6, waiting for transfers between devices  30.5 us
    all_to_all x1, waiting for transfers between devices, shards(): lax.all_to_all(spread, 'expert', split_axis=1, concat_axis=0, tiled=True)  25 us
    reduce_scatter x1, waiting for transfers between devices, shards(): lax.psum_scatter(head_terms, 'expert', scatter_dimension=0, tiled=True)  19.3 us
    dot_general x1, matrix products, expert_rows(): jnp.einsum('nef,efd->ned', hidden, w_down, preferred_element_type=jnp.flo...  14.2 us
  transfers between devices with their start and end apart: 8, of which 7 were waited for; matrix products, arithmetic and copies ran while one was open for 2% of the time, Pallas kernels for 0%

commit v1 on v0

--- a/solution.py
+++ b/solution.py
@@ -110,7 +110,9 @@
         lax.all_to_all(partner.T, "expert", split_axis=0, concat_axis=1, tiled=True),
     )
     present = (arrived_partner >= 0).astype(jnp.int32)
-    position = jnp.cumsum(present, axis=1) - 1
+    slots = jnp.arange(present.shape[1])
+    earlier = slots[:, None] < slots[None, :]
+    position = jnp.sum(jnp.where(earlier[None], present[:, :, None], 0), axis=1)
     picker = (present[:, None, :] > 0) & (
         position[:, None, :] == jnp.arange(GROUP_CAP)[None, :, None]
     )

time: 526 us -> 526 us (level)
  no operation moved by 1% of the time
where the time goes in v1:
time: 526 us; the launch traced here: 525 us
  waiting for transfers between devices  391 us (74%)
  matrix products  59 us (11%)
  blocking collectives  36.4 us (7%)
  between operations  14.2 us (3%)
  starting transfers between devices  11.1 us (2%)
  local copies, waits for them, and re-layouts  8.8 us (2%)
    all_gather x1, waiting for transfers between devices, shards(): lax.all_gather(out_weight, 'dp', axis=1, tiled=True)  125 us
    reduce_scatter x1, waiting for transfers between devices, shards(): lax.psum_scatter(expert_rows(gathered, w_gate, w_up, w_down), 'dp', scatt...  117 us
    all_gather x1, waiting for transfers between devices, shards(): gathered = lax.all_gather(compact, 'dp', axis=0, tiled=True)  60.4 us
    all_gather x1, blocking collectives, shards(): everyone = lax.all_gather(summary, 'dp', axis=0, tiled=True)  30.6 us
    unnamed x6, waiting for transfers between devices  30.5 us
    all_to_all x1, waiting for transfers between devices, shards(): lax.all_to_all(spread, 'expert', split_axis=1, concat_axis=0, tiled=True)  25 us
    reduce_scatter x1, waiting for transfers between devices, shards(): lax.psum_scatter(head_terms, 'expert', scatter_dimension=0, tiled=True)  19.3 us
    dot_general x1, matrix products, expert_rows(): jnp.einsum('nef,efd->ned', hidden, w_down, preferred_element_type=jnp.flo...  14.2 us
  transfers between devices with their start and end apart: 8, of which 7 were waited for; matrix products, arithmetic and copies ran while one was open for 2% of the time, Pallas kernels for 0%

profile of v1, /device:TPU:0, one launch (start us, length us, event | category | flops | bytes accessed | tf_op | source)
XLA Modules:
  0.0 525.4 jit_solution(7493323034946388113)
XLA Ops:
  7.2 0.0 copy-start
  7.2 0.0 all-gather.4.cloned.1.call-start
  7.3 0.7 all-gather.4.cloned.1.call-update
  7.9 0.0 reduce-scatter.6.cloned.1.call-start
  8.0 1.0 reshape.252
  9.0 1.3 reshape.251
  10.4 0.3 reshape.254
  10.7 0.3 fusion.43
  11.0 0.5 bitcast_reduce_fusion
  11.6 0.1 fusion.19
  11.6 0.5 fusion.5
  12.2 0.8 fusion.14
  13.0 0.3 fusion.9
  13.2 0.1 copy.76
  13.3 0.1 reshape.256
  13.4 0.0 copy-start.10
  13.4 0.0 copy-start.3
  13.4 124.8 %all-gather.4.cloned.1.call-done = bf16[1024,4096]{1,0:T(8,128)(2,1)} async-done(((bf16[1024,512]{1,0:T(8,128)(2,1)}), bf16[1024,4096]{1,0:T(8,128)(2,1)}) %all-gather.4.cloned.1.call-update) | async-done | bytes 8388624 | tf_op jit(solution)/shard_map/all_gather | solution.py:91
  138.2 6.0 %fusion.49 = f32[64,4096]{1,0:T(8,128)} fusion(bf16[64,1024]{1,0:T(8,128)(2,1)S(1)} %reshape.256, bf16[1024,4096]{1,0:T(8,128)(2,1)} %all-gather.4.cloned.1.call-done), kind=kOutput, calls=%fused_computation.95 | convolution fusion | flops 536870912 | bytes 9568256 | tf_op jit(solution)/shard_map/dot_general | solution.py:89
  144.2 0.0 reduce-scatter.6.cloned.1.call-update
  144.3 0.7 compare_select_fusion.1
  145.0 3.2 all-to-all-start
  148.2 19.3 %reduce-scatter.6.cloned.1.call-done = f32[16,4096]{1,0:T(8,128)} async-done(((f32[64,4096]{1,0:T(8,128)}), f32[16,4096]{1,0:T(8,128)}) %reduce-scatter.6.cloned.1.call-update) | async-done | bytes 262160 | tf_op jit(solution)/shard_map/reduce_scatter | solution.py:94
  167.5 1.1 multiply_reduce_fusion
  168.6 1.0 multiply_convert_fusion.1
  169.7 1.1 broadcast_select_fusion
  170.8 3.5 all-to-all-start.1
  174.3 0.0 all-gather.6.cloned.1.call-start
  174.4 0.1 reshape.259
  174.5 0.1 select_reduce_fusion
  174.6 14.1 %all-to-all-done.1 = bf16[8,16,4096]{2,1,0:T(8,128)(2,1)S(1)} async-done(((bf16[8,16,4096]{2,1,0:T(8,128)(2,1)}), bf16[8,16,4096]{2,1,0:T(8,128)(2,1)S(1)}, u32[]{:S(2)}, u32[]{:S(2)}) %all-to-all-start.1) | async-done | bytes 1048608 | tf_op jit(solution)/shard_map/all_to_all | solution.py:109
  188.7 0.1 copy.78
  188.8 1.0 fusion.1
  189.9 0.0 all-gather.6.cloned.1.call-update
  189.9 0.2 reduce-scatter.8.cloned.1.call-start
  190.1 60.4 %all-gather.6.cloned.1.call-done = bf16[192,2,4096]{2,0,1:T(8,128)(2,1)} async-done(((bf16[24,2,4096]{2,0,1:T(8,128)(2,1)}), bf16[192,2,4096]{2,0,1:T(8,128)(2,1)}) %all-gather.6.cloned.1.call-update) | async-done | bytes 3145744 | tf_op jit(solution)/shard_map/all_gather | solution.py:127
  250.5 13.9 %convolution_bitcast_fusion.3 = f32[192,2,1792]{2,0,1:T(8,128)S(1)} fusion(bf16[192,2,4096]{2,0,1:T(8,128)(2,1)} %all-gather.6.cloned.1.call-done, bf16[2,4096,1792]{2,1,0:T(8,128)(2,1)} %param.26), kind=kOutput, calls=%fused_computation.6 | convolution fusion | flops 5637144576 | bytes 35258368 | tf_op jit(solution)/shard_map/ned,edf->nef/dot_general | solution.py:56
  264.4 12.5 %multiply_convert_fusion = bf16[192,2,1792]{2,0,1:T(8,128)(2,1)S(1)} fusion(f32[192,2,1792]{2,0,1:T(8,128)S(1)} %convolution_bitcast_fusion.3, bf16[192,2,4096]{2,0,1:T(8,128)(2,1)S(1)} %copy-done.1, bf16[2,4096,1792]{2,1,0:T(8,128)(2,1)} %param.27), kind=kOutput, calls=%fused_computation.7 | convolution fusion | flops 5641273344 | bytes 36634624 | tf_op jit(solution)/shard_map/ned,edf->nef/dot_general | solution.py:57
  276.9 14.2 %convolution_bitcast_fusion = f32[192,2,4096]{2,0,1:T(8,128)} fusion(bf16[192,2,1792]{2,0,1:T(8,128)(2,1)S(1)} %multiply_convert_fusion, bf16[2,1792,4096]{2,1,0:T(8,128)(2,1)} %param.28), kind=kOutput, calls=%fused_computation.1 | convolution fusion | flops 5637144576 | bytes 37027840 | tf_op jit(solution)/shard_map/nef,efd->ned/dot_general | solution.py:59
  291.2 0.0 reduce-scatter.8.cloned.1.call-update
  291.2 116.7 %reduce-scatter.8.cloned.1.call-done = f32[24,2,4096]{2,0,1:T(8,128)} async-done(((f32[192,2,4096]{2,0,1:T(8,128)}), f32[24,2,4096]{2,0,1:T(8,128)}) %reduce-scatter.8.cloned.1.call-update) | async-done | bytes 786448 | tf_op jit(solution)/shard_map/reduce_scatter | solution.py:128
  407.9 2.2 fusion.29
  410.1 3.0 copy.79
  413.0 3.7 all-to-all-start.2
  416.8 0.3 reduce-scatter.10.cloned.1.call-start
  417.1 0.1 dynamic_slice.3
  417.2 0.2 select_reduce_fusion.2
  417.4 0.1 copy.90
  417.4 25.0 %all-to-all-done.2 = f32[2,64,4096]{2,0,1:T(2,128)S(1)} async-done(((f32[2,64,4096]{2,0,1:T(2,128)}), f32[2,64,4096]{2,0,1:T(2,128)S(1)}, u32[]{:S(2)}, u32[]{:S(2)}) %all-to-all-start.2) | async-done | bytes 2097184 | tf_op jit(solution)/shard_map/all_to_all | solution.py:134
  442.4 1.2 copy.80
  443.7 0.2 copy.81
  443.9 2.9 fusion.3
  446.8 3.2 convolution_bitcast_fusion.1
  449.9 0.0 reduce-scatter.10.cloned.1.call-update
  450.0 0.1 broadcast_compare_fusion
  450.0 29.7 %reduce-scatter.10.cloned.1.call-done = f32[1024,2]{1,0:T(8,128)} async-done(((f32[4096,2]{1,0:T(8,128)}), f32[1024,2]{1,0:T(8,128)}) %reduce-scatter.10.cloned.1.call-update) | async-done | bytes 8208
  479.8 1.2 copy.102
  481.0 0.1 multiply_reduce_fusion.1
  481.1 5.8 %psum.7 = f32[2]{0:T(128)S(1)} all-reduce(f32[2]{0:T(128)S(1)} %multiply_reduce_fusion.1), channel_id=1, replica_groups=mesh['dp'=8,'expert'=4] {'expert'}, use_global_device_ids=true, to_apply=%region_12.13 | all-reduce | flops 2 | bytes 16 | tf_op jit(solution)/shard_map/psum | solution.py:142
  486.9 0.1 fusion.63
  487.0 0.1 multiply_convert_fusion.2
  487.1 30.6 %all-gather = bf16[8,2,1024]{2,1,0:T(2,128)(2,1)S(1)} all-gather(bf16[1,2,1024]{2,1,0:T(2,128)(2,1)S(1)} %fusion.63), channel_id=1, replica_groups=mesh['dp'=8,'expert'=4] {'dp'}, dimensions={0}, use_global_device_ids=true | all-gather | bytes 36864 | tf_op jit(solution)/shard_map/all_gather | solution.py:146
  517.7 0.3 fusion.44
  518.0 0.8 fusion.13
  (43 shorter events, 0.2 us)
Async XLA Ops:
  7.2 410.0 %copy-start = (bf16[4096,8]{0,1:T(8,128)(2,1)S(1)}, bf16[4096,8]{0,1:T(8,128)(2,1)}, u32[]{:S(2)}) copy-start(bf16[4096,8]{0,1:T(8,128)(2,1)} %param.24) | copy-start | bytes 196612
  7.2 3.1 copy-start.5
  7.2 3.2 copy-start.4
  7.2 3.5 copy-start.6
  7.2 131.0 %all-gather.4.cloned.1.call-start = ((), (), s32[]{:S(2)}) async-start(), calls=%async_computation.6 | async-start | bytes 9437184 | tf_op jit(solution)/shard_map/all_gather | solution.py:91
  7.9 159.5 %reduce-scatter.6.cloned.1.call-start = ((), (), s32[]{:S(2)}) async-start(), calls=%async_computation.7 | async-start | bytes 1310720 | tf_op jit(solution)/shard_map/reduce_scatter | solution.py:94
  13.4 130.9 %copy-start.10 = (s32[16,2]{0,1:T(2,128)S(1)}, s32[16,2]{0,1:T(2,128)}, u32[]{:S(2)}) copy-start(s32[16,2]{0,1:T(2,128)} %param.25) | copy-start | bytes 388
  13.4 154.1 %copy-start.3 = (bf16[16,4096]{1,0:T(8,128)(2,1)S(1)}, bf16[16,4096]{1,0:T(8,128)(2,1)}, u32[]{:S(2)}) copy-start(bf16[16,4096]{1,0:T(8,128)(2,1)} %param.16) | copy-start | bytes 393220
  13.4 155.2 %copy-start.7 = (f32[4096]{0:T(1024)S(1)}, f32[4096]{0:T(1024)}, u32[]{:S(2)}) copy-start(f32[4096]{0:T(1024)} %param.23) | copy-start | bytes 49156
  145.0 25.8 %all-to-all-start = ((s32[4,2,16]{2,1,0:T(2,128)}), s32[4,2,16]{2,1,0:T(2,128)S(1)}, u32[]{:S(2)}, u32[]{:S(2)}) async-start(s32[4,2,16]{2,1,0:T(2,128)} %compare_select_fusion.1), calls=%async_computation.1 | async-start | bytes 8192 | tf_op jit(solution)/shard_map/all_to_all | solution.py:110
  170.8 18.0 %all-to-all-start.1 = ((bf16[8,16,4096]{2,1,0:T(8,128)(2,1)}), bf16[8,16,4096]{2,1,0:T(8,128)(2,1)S(1)}, u32[]{:S(2)}, u32[]{:S(2)}) async-start(bf16[8,16,4096]{2,1,0:T(8,128)(2,1)} %broadcast_select_fusion), calls=%async_computation.2 | async-start | bytes 2097152 | tf_op jit(solution)/shard_map/all_to_all | solution.py:109
  174.3 76.2 %all-gather.6.cloned.1.call-start = ((), (), s32[]{:S(2)}) async-start(), calls=%async_computation.8 | async-start | bytes 3538944 | tf_op jit(solution)/shard_map/all_gather | solution.py:127
  189.9 218.0 %reduce-scatter.8.cloned.1.call-start = ((), (), s32[]{:S(2)}) async-start(), calls=%async_computation.9 | async-start | bytes 7077888 | tf_op jit(solution)/shard_map/reduce_scatter | solution.py:128
  250.5 13.9 %copy-start.1 = (bf16[192,2,4096]{2,0,1:T(8,128)(2,1)S(1)}, bf16[192,2,4096]{2,0,1:T(8,128)(2,1)}, u32[]{:S(2)}) copy-start(bf16[192,2,4096]{2,0,1:T(8,128)(2,1)} %all-gather.6.cloned.1.call-done) | copy-start | bytes 9437188
  413.0 4.0 copy-start.11
  413.0 29.4 %all-to-all-start.2 = ((f32[2,64,4096]{2,0,1:T(2,128)}), f32[2,64,4096]{2,0,1:T(2,128)S(1)}, u32[]{:S(2)}, u32[]{:S(2)}) async-start(f32[2,64,4096]{2,0,1:T(2,128)} %copy.79), calls=%async_computation.4 | async-start | bytes 4194304 | tf_op jit(solution)/shard_map/all_to_all | solution.py:134
  416.8 63.0 %reduce-scatter.10.cloned.1.call-start = ((), (), s32[]{:S(2)}) async-start(), calls=%async_computation.10 | async-start | bytes 2621440
  443.7 3.1 copy-start.2
  446.7 34.4 %copy-start.12 = (f32[8]{0:T(128)S(1)}, f32[8]{0:T(128)}, u32[]{:S(2)}) copy-start(f32[8]{0:T(128)} %param.30) | copy-start | bytes 100
  446.8 40.2 %copy-start.8 = (f32[1024]{0:T(1024)S(1)}, f32[1024]{0:T(1024)}, u32[]{:S(2)}) copy-start(f32[1024]{0:T(1024)} %param.29) | copy-start | bytes 12292
  487.1 31.8 %copy-start.9 = (bf16[2,1024]{1,0:T(2,128)(2,1)}, bf16[2,1024]{1,0:T(2,128)(2,1)S(1)}, u32[]{:S(2)}) copy-start(bf16[2,1024]{1,0:T(2,128)(2,1)S(1)} %multiply_convert_fusion.2) | copy-start | bytes 12292
Sparse Core Ops, SparseCore 0:
  10.1 128.0 all-gather.3
  144.4 23.0 reduce-scatter.5
  190.0 60.4 all-gather.5
  291.3 116.5 reduce-scatter.7
  450.1 29.6 reduce-scatter.9

commit v2 on v0

v2 whole, which is shorter than its diff:
```python
import math

import jax
import jax.numpy as jnp
from jax import lax
from jax.sharding import PartitionSpec as P

HEADS = 32
KVH = 8
HD = 128
EXPERTS = 8
WIN = 32
GROUP_CAP = 24


EPSILON = 1e-05


def attend(queries, new_keys, new_values, cache_keys, cache_values):
    span_count, cache_len, kv_width = cache_keys.shape
    kv_local = kv_width // HD
    group = HEADS // KVH
    window = queries.shape[0] // span_count
    query_view = queries.reshape(span_count, window, kv_local, group, HD)
    fresh_keys = new_keys.reshape(span_count, window, kv_local, HD)
    fresh_values = new_values.reshape(span_count, window, kv_local, HD)
    stored_keys = cache_keys.reshape(span_count, cache_len, kv_local, HD)
    stored_values = cache_values.reshape(span_count, cache_len, kv_local, HD)
    factor = 1.0 / math.sqrt(HD)
    past_scores = (
        jnp.einsum("ctkgd,cpkd->ckgtp", query_view, stored_keys, preferred_element_type=jnp.float32)
        * factor
    )
    fresh_scores = (
        jnp.einsum("ctkgd,cskd->ckgts", query_view, fresh_keys, preferred_element_type=jnp.float32)
        * factor
    )
    causal = jnp.arange(window)[:, None] >= jnp.arange(window)[None, :]
    fresh_scores = jnp.where(causal, fresh_scores, -jnp.inf)
    highest = jnp.maximum(jnp.max(past_scores, axis=-1), jnp.max(fresh_scores, axis=-1))[..., None]
    past_exp = jnp.exp(past_scores - highest)
    fresh_exp = jnp.exp(fresh_scores - highest)
    totals = jnp.sum(past_exp, axis=-1, keepdims=True) + jnp.sum(fresh_exp, axis=-1, keepdims=True)
    past_weights = (past_exp / totals).astype(jnp.bfloat16)
    fresh_weights = (fresh_exp / totals).astype(jnp.bfloat16)
    context = jnp.einsum(
        "ckgtp,cpkd->ctkgd", past_weights, stored_values, preferred_element_type=jnp.float32
    )
    context = context + jnp.einsum(
        "ckgts,cskd->ctkgd", fresh_weights, fresh_values, preferred_element_type=jnp.float32
    )
    return context.astype(jnp.bfloat16).reshape(span_count * window, kv_local * group * HD)


def shards(
    residual,
    queries,
    new_keys,
    new_values,
    cache_keys,
    cache_values,
    out_weight,
    ffn_gain,
    router,
    routes,
    w_gate,
    w_up,
    w_down,
    summary_gain,
    reduce_scale,
    assign,
):
    n_dp, n_ex = lax.axis_size("dp"), lax.axis_size("expert")
    dp_index, column = lax.axis_index("dp"), lax.axis_index("expert")
    both = ("dp", "expert")
    span_local = cache_keys.shape[0]
    tok_local, width = residual.shape
    tokens = tok_local * n_dp * n_ex
    spans = span_local * n_dp
    exact = lax.Precision.HIGHEST
    all_routes = lax.all_gather(routes, both, axis=0, tiled=True)
    attended = attend(queries, new_keys, new_values, cache_keys, cache_values)
    rows = lax.all_gather(attended, "dp", axis=0, tiled=True)
    parts = jnp.dot(rows, out_weight, preferred_element_type=jnp.float32).astype(jnp.bfloat16)
    parts = lax.all_to_all(
        parts.reshape(n_dp * n_ex, tok_local, -1), both, split_axis=0, concat_axis=0, tiled=True
    )
    terms = jnp.sum(parts.reshape(n_dp, n_ex, tok_local, -1).astype(jnp.float32), axis=1)
    mixed = residual.astype(jnp.float32) + terms.transpose(1, 0, 2).reshape(tok_local, width)
    normed = (
        mixed * lax.rsqrt(jnp.mean(mixed * mixed, axis=-1, keepdims=True) + EPSILON) * ffn_gain
    ).astype(jnp.bfloat16)
    everyone = lax.all_gather(normed, both, axis=0, tiled=True)
    ex_local = w_gate.shape[0]
    capacity = n_dp * GROUP_CAP
    own = column * ex_local + jnp.arange(ex_local, dtype=jnp.int32)
    is_first = all_routes[None, :, 0] == own[:, None]
    is_second = all_routes[None, :, 1] == own[:, None]
    member = is_first | is_second
    index = jnp.arange(tokens)
    earlier = (index[:, None] < index[None, :]).astype(jnp.bfloat16)
    place = jnp.dot(
        member.astype(jnp.bfloat16), earlier, preferred_element_type=jnp.float32
    ).astype(jnp.int32)
    picker = member[:, None, :] & (place[:, None, :] == jnp.arange(capacity)[None, :, None])
    compact = jnp.dot(
        picker.astype(jnp.bfloat16).reshape(ex_local * capacity, tokens),
        everyone,
        preferred_element_type=jnp.float32,
    ).astype(jnp.bfloat16)
    compact = compact.reshape(ex_local, capacity, width)
    logits = jnp.dot(everyone, router, preferred_element_type=jnp.float32)
    ids = jnp.arange(EXPERTS, dtype=jnp.int32)
    first_logit = jnp.sum(jnp.where(all_routes[:, 0:1] == ids, logits, 0.0), axis=-1)
    second_logit = jnp.sum(jnp.where(all_routes[:, 1:2] == ids, logits, 0.0), axis=-1)
    gates = jnp.where(
        is_first,
        jax.nn.sigmoid(first_logit - second_logit)[None],
        jnp.where(is_second, jax.nn.sigmoid(second_logit - first_logit)[None], 0.0),
    )
    slot_gate = jnp.sum(jnp.where(picker, gates[:, None, :], 0.0), axis=-1)
    slot_span = jnp.sum(jnp.where(picker, index // WIN, 0), axis=-1)
    pool = jnp.where(
        slot_span[:, None, :] == jnp.arange(spans)[None, :, None], slot_gate[:, None, :], 0.0
    )
    gate_proj = jnp.einsum("end,edf->enf", compact, w_gate, preferred_element_type=jnp.float32)
    up_proj = jnp.einsum("end,edf->enf", compact, w_up, preferred_element_type=jnp.float32)
    hidden = (jax.nn.silu(gate_proj) * up_proj).astype(jnp.bfloat16)
    weighed = jnp.einsum("esn,enf->sef", pool, hidden.astype(jnp.float32), precision=exact)
    weighed = weighed.reshape(spans, -1)
    high = lax.reduce_precision(weighed, 8, 7)
    halves = jnp.concatenate([high, weighed - high], axis=0).astype(jnp.bfloat16)
    down = jnp.dot(halves, w_down.reshape(-1, width), preferred_element_type=jnp.float32)
    token_span = ((dp_index * n_ex + column) * tok_local + jnp.arange(tok_local)) // WIN
    pool_matrix = (token_span[None, :] == jnp.arange(spans)[:, None]).astype(jnp.float32)
    pooled = down[:spans] + down[spans:] + jnp.dot(pool_matrix, mixed, precision=exact)
    pooled = lax.all_to_all(
        pooled.reshape(spans, n_ex, -1).transpose(1, 0, 2),
        "expert",
        split_axis=0,
        concat_axis=0,
        tiled=True,
    )
    pooled = lax.psum(jnp.sum(pooled, axis=0), "dp")
    squares = lax.psum(jnp.sum(pooled * pooled, axis=-1), "expert")
    summary = (pooled * lax.rsqrt(squares / width + EPSILON)[:, None] * summary_gain).astype(
        jnp.bfloat16
    )
    heads_local = summary.shape[1] // HD
    others = summary.reshape(spans, heads_local, HD)
    summary = lax.dynamic_slice_in_dim(summary, dp_index * span_local, span_local)
    mine = summary.reshape(span_local, heads_local, HD)
    factor = reduce_scale / math.sqrt(HD)
    scores = (
        jnp.einsum("chd,khd->hck", mine, others, preferred_element_type=jnp.float32)
        * factor[:, None, None]
    )
    own_assign = lax.dynamic_slice_in_dim(assign, dp_index * span_local, span_local)
    same = own_assign[:, None] == assign[None, :]
    scores = jnp.where(same[None], scores, -jnp.inf)
    highest = jnp.max(scores, axis=-1, keepdims=True)
    expo = jnp.exp(scores - highest)
    weights = (expo / jnp.sum(expo, axis=-1, keepdims=True)).astype(jnp.bfloat16)
    reduced = jnp.einsum("hck,khd->chd", weights, others, preferred_element_type=jnp.float32)
    reduced = reduced.reshape(span_local, heads_local * HD).astype(jnp.bfloat16)
    return (summary, reduced)


def solution(mesh):
    return jax.shard_map(
        shards,
        mesh=mesh,
        in_specs=(
            P(("dp", "expert"), None),
            P("dp", "expert"),
            P("dp", "expert"),
            P("dp", "expert"),
            P("dp", None, "expert"),
            P("dp", None, "expert"),
            P("expert", "dp"),
            P(),
            P(),
            P(("dp", "expert"), None),
            P("expert", None, "dp"),
            P("expert", None, "dp"),
            P("expert", "dp", None),
            P("expert"),
            P("expert"),
            P(),
        ),
        out_specs=(P("dp", "expert"), P("dp", "expert")),
        check_vma=False,
    )
```

time: 526 us -> 286 us (0.54)
  waiting for transfers between devices: 391 us -> 136 us
  blocking collectives: 36.4 us -> 63.7 us
  starting transfers between devices: 11.1 us -> 3.53 us
  matrix products: 59 us -> 52.5 us
    reduce_scatter x2 -> x0, waiting for transfers between devices: 136 us -> none  [the longest x1 117 us: shards(): lax.psum_scatter(expert_rows(gathered, w_gate, w_up, w_down), 'dp', scatt...]
    all_gather x2, waiting for transfers between devices: 185 us -> 63.4 us  [the longest x1 43 us: shards(): rows = lax.all_gather(attended, 'dp', axis=0, tiled=True)]
    psum x0 -> x1, waiting for transfers between devices: none -> 67.2 us  [shards(): pooled = lax.psum(jnp.sum(pooled, axis=0), 'dp')]
    all_to_all x3 -> x1, waiting for transfers between devices: 39 us -> 5.88 us  [shards(): lax.all_to_all(pooled.reshape(spans, n_ex, -1).transpose(1, 0, 2), 'exper...]
    unnamed x6 -> x3, waiting for transfers between devices: 30.5 us -> 0.05 us
    all_to_all x0 -> x1, blocking collectives: none -> 18.7 us  [shards(): lax.all_to_all(parts.reshape(n_dp * n_ex, tok_local, -1), both, split_axi...]
    all_gather x1, blocking collectives: 30.6 us -> 39.3 us  [shards(): all_routes = lax.all_gather(routes, both, axis=0, tiled=True)]
    dot_general x8 -> x9, matrix products: 52.9 us -> 45.4 us  [the longest x1 12.5 us: shards(): jnp.einsum('end,edf->enf', compact, w_up, preferred_element_type=jnp.floa...]
  transfers between devices with their start and end apart: 8 -> 4, of which waited for: 7 -> 4; matrix products, arithmetic and copies ran while one was open for 2% -> 0% of each run, Pallas kernels for 0% -> 0%
where the time goes in v2:
time: 286 us; the launch traced here: 285 us
  waiting for transfers between devices  136 us (48%)
  blocking collectives  63.7 us (22%)
  matrix products  52.5 us (18%)
  between operations  14.1 us (5%)
  local copies, waits for them, and re-layouts  9.4 us (3%)
  other arithmetic  5.07 us (2%)
  starting transfers between devices  3.53 us (1%)
    psum x1, waiting for transfers between devices, shards(): pooled = lax.psum(jnp.sum(pooled, axis=0), 'dp')  67.2 us
    all_gather x1, waiting for transfers between devices, shards(): rows = lax.all_gather(attended, 'dp', axis=0, tiled=True)  43 us
    all_gather x1, blocking collectives, shards(): all_routes = lax.all_gather(routes, both, axis=0, tiled=True)  39.3 us
    all_gather x1, waiting for transfers between devices, shards(): everyone = lax.all_gather(normed, both, axis=0, tiled=True)  20.4 us
    all_to_all x1, blocking collectives, shards(): lax.all_to_all(parts.reshape(n_dp * n_ex, tok_local, -1), both, split_axi...  18.7 us
    dot_general x1, matrix products, shards(): jnp.einsum('end,edf->enf', compact, w_up, preferred_element_type=jnp.floa...  12.5 us
    dot_general x1, matrix products, shards(): jnp.einsum('end,edf->enf', compact, w_gate, preferred_element_type=jnp.fl...  12.4 us
    dot_general x1, matrix products, shards(): jnp.dot(halves, w_down.reshape(-1, width), preferred_element_type=jnp.flo...  12.1 us
  transfers between devices with their start and end apart: 4, of which 4 were waited for; matrix products, arithmetic and copies ran while one was open for 0% of the time, Pallas kernels for 0%

profile of v2, /device:TPU:0, one launch (start us, length us, event | category | flops | bytes accessed | tf_op | source)
XLA Modules:
  0.0 284.7 jit_solution(1026519979868802233)
XLA Ops:
  7.2 0.0 copy-start
  7.2 0.0 all-gather.4.cloned.1.call-start
  7.2 1.1 reshape.277
  8.3 2.2 reshape.276
  10.5 1.4 reshape.278
  11.8 1.8 bitcast_reduce_fusion
  13.6 0.3 fusion.47
  13.9 0.5 fusion.2
  14.5 0.1 fusion.17
  14.5 2.2 reshape.279
  16.7 0.8 reshape.280
  17.5 1.9 fusion.11
  19.4 0.2 fusion.6
  19.7 0.1 copy.74
  19.7 0.7 reshape.281
  20.5 0.0 all-gather.4.cloned.1.call-update
  20.5 0.0 copy-start.3
  20.5 0.0 copy-start.6
  20.5 0.0 copy-start.9
  20.5 0.0 all-gather.6.cloned.1.call-start
  20.6 43.0 %all-gather.4.cloned.1.call-done = bf16[512,1024]{1,0:T(8,128)(2,1)} async-done(((bf16[64,1024]{1,0:T(8,128)(2,1)}), bf16[512,1024]{1,0:T(8,128)(2,1)}) %all-gather.4.cloned.1.call-update) | async-done | bytes 1048592 | tf_op jit(solution)/shard_map/all_gather | solution.py:83
  63.6 1.9 convolution_convert_fusion.1
  65.5 0.0 copy-start.10
  65.5 0.0 copy-start.5
  65.5 18.7 %all_to_all.10 = bf16[32,16,512]{2,1,0:T(8,128)(2,1)S(1)} all-to-all(bf16[32,16,512]{2,1,0:T(8,128)(2,1)S(1)} %bitcast.98), channel_id=1, replica_groups=mesh['dp'=8,'expert'=4] {'dp','expert'}, dimensions={0} | all-to-all | bytes 1048576 | tf_op jit(solution)/shard_map/all_to_all | solution.py:85
  84.2 0.1 convert_reduce_fusion
  84.4 0.2 multiply_reduce_fusion
  84.5 0.7 multiply_convert_fusion.1
  85.3 0.0 all-gather.6.cloned.1.call-update
  85.3 39.3 %all-gather = s32[32,16,2]{1,2,0:T(2,128)S(1)} all-gather(s32[1,16,2]{1,2,0:T(2,128)S(1)} %bitcast.107), channel_id=1, replica_groups=mesh['dp'=8,'expert'=4] {'dp','expert'}, dimensions={0}, use_global_device_ids=true | all-gather | bytes 4224 | tf_op jit(solution)/shard_map/all_gather | solution.py:81
  124.6 0.1 reshape.292
  124.7 0.1 eq.145
  124.8 0.1 compare_or_fusion
  124.9 0.2 convolution_convert_fusion.3
  125.1 0.2 fusion.16
  125.3 0.1 dynamic_slice.7
  125.4 0.2 select_reduce_fusion.1
  125.6 20.4 %all-gather.6.cloned.1.call-done = bf16[512,4096]{1,0:T(8,128)(2,1)} async-done(((bf16[16,4096]{1,0:T(8,128)(2,1)}), bf16[512,4096]{1,0:T(8,128)(2,1)}) %all-gather.6.cloned.1.call-update) | async-done | bytes 4194320 | tf_op jit(solution)/shard_map/all_gather | solution.py:93
  146.0 3.5 %select_reduce_fusion.3 = (f32[512]{0:T(512)S(1)}, f32[512]{0:T(512)S(1)}) fusion(s32[512]{0:T(512)S(1)} %bitcast.101, s32[512]{0:T(512)S(1)} %bitcast.104, bf16[512,4096]{1,0:T(8,128)(2,1)} %all-gather.6.cloned.1.call-done, bf16[4096,8]{0,1:T(8,128)(2,1)S(1)} %copy-done.5), kind=kOutput, calls=%fused_computation.69 | convolution fusion | flops 33577984 | bytes 4268032 | tf_op jit(solution)/shard_map/dot_general | solution.py:112
  149.6 0.1 compare_select_fusion.1
  149.7 0.2 select_reduce_fusion
  149.9 1.8 convolution_convert_fusion
  151.7 12.4 %fusion.53 = f32[2,192,1792]{2,1,0:T(8,128)S(1)} fusion(bf16[2,192,4096]{2,1,0:T(8,128)(2,1)S(1)} %bitcast.88, bf16[2,4096,1792]{2,1,0:T(8,128)(2,1)} %param.26), kind=kOutput, calls=%fused_computation.106 | convolution fusion | flops 5637144576 | bytes 35258368 | tf_op jit(solution)/shard_map/end,edf->enf/dot_general | solution.py:126
  164.2 12.5 %multiply_convert_fusion = bf16[2,192,1792]{2,1,0:T(8,128)(2,1)S(1)} fusion(f32[2,192,1792]{2,1,0:T(8,128)S(1)} %fusion.53, bf16[2,192,4096]{2,1,0:T(8,128)(2,1)S(1)} %bitcast.89, bf16[2,4096,1792]{2,1,0:T(8,128)(2,1)} %param.27), kind=kOutput, calls=%fused_computation.3 | convolution fusion | flops 5641273344 | bytes 36634624 | tf_op jit(solution)/shard_map/end,edf->enf/dot_general | solution.py:127
  176.7 0.6 convolution_bitcast_fusion
  177.4 0.0 copy-start.11
  177.4 0.0 copy-start.7
  177.4 0.0 copy-start.1
  177.4 12.1 %fusion.19 = f32[32,4096]{1,0:T(8,128)S(1)} fusion(bf16[3584,4096]{1,0:T(8,128)(2,1)} %bitcast.87, bf16[16,3584]{1,0:T(8,128)(2,1)S(1)} %get-tuple-element.5, bf16[16,3584]{1,0:T(8,128)(2,1)S(1)} %get-tuple-element.4), kind=kOutput, calls=%fused_computation.47 | convolution fusion | flops 939982848 | bytes 30113792 | tf_op jit(solution)/shard_map/dot_general | solution.py:133
  189.5 0.3 convolution_add_fusion
  189.8 0.7 copy.128
  190.5 3.4 %all-to-all-start.1 = ((f32[4,16,1024]{2,1,0:T(8,128)}), f32[4,16,1024]{2,1,0:T(8,128)S(1)}, u32[]{:S(2)}, u32[]{:S(2)}) async-start(f32[4,16,1024]{2,1,0:T(8,128)} %bitcast.86), calls=%async_computation.1 | async-start | bytes 524288 | tf_op jit(solution)/shard_map/all_to_all | solution.py:137
  193.9 0.0 all-reduce.2.cloned.1.call-start
  194.0 0.1 broadcast_compare_fusion
  194.1 5.9 %all-to-all-done.1 = f32[4,16,1024]{2,1,0:T(8,128)S(1)} async-done(((f32[4,16,1024]{2,1,0:T(8,128)}), f32[4,16,1024]{2,1,0:T(8,128)S(1)}, u32[]{:S(2)}, u32[]{:S(2)}) %all-to-all-start.1) | async-done | bytes 262176 | tf_op jit(solution)/shard_map/all_to_all | solution.py:137
  199.9 0.6 reduce_sum.107
  200.6 0.0 all-reduce.2.cloned.1.call-update
  200.6 67.2 %all-reduce.2.cloned.1.call-done = f32[16,1024]{1,0:T(8,128)} async-done(((f32[16,1024]{1,0:T(8,128)}), f32[16,1024]{1,0:T(8,128)}) %all-reduce.2.cloned.1.call-update) | async-done | bytes 65552 | tf_op jit(solution)/shard_map/psum | solution.py:144
  267.8 1.0 multiply_reduce_fusion.1
  268.8 5.7 %psum.15 = f32[16]{0:T(128)S(1)} all-reduce(f32[16]{0:T(128)S(1)} %multiply_reduce_fusion.1), channel_id=1, replica_groups=mesh['dp'=8,'expert'=4] {'expert'}, use_global_device_ids=true, to_apply=%region_13.14 | all-reduce | flops 16 | bytes 128 | tf_op jit(solution)/shard_map/psum | solution.py:145
  274.4 0.9 multiply_convert_fusion.2
  275.4 0.0 copy-start.8
  275.4 1.2 fusion.48
  276.6 1.6 fusion.10
  (31 shorter events, 0.2 us)
Async XLA Ops:
  7.2 56.4 %copy-start = (bf16[1024,512]{1,0:T(8,128)(2,1)S(1)}, bf16[1024,512]{1,0:T(8,128)(2,1)}, u32[]{:S(2)}) copy-start(bf16[1024,512]{1,0:T(8,128)(2,1)} %param.22) | copy-start | bytes 3145732
  7.2 56.4 %all-gather.4.cloned.1.call-start = ((), (), s32[]{:S(2)}) async-start(), calls=%async_computation.2 | async-start | bytes 1179648 | tf_op jit(solution)/shard_map/all_gather | solution.py:83
  11.8 1.8 copy-start.4
  20.5 63.9 %copy-start.3 = (bf16[16,4096]{1,0:T(8,128)(2,1)S(1)}, bf16[16,4096]{1,0:T(8,128)(2,1)}, u32[]{:S(2)}) copy-start(bf16[16,4096]{1,0:T(8,128)(2,1)} %param.16) | copy-start | bytes 393220
  20.5 64.0 %copy-start.6 = (f32[4096]{0:T(1024)S(1)}, f32[4096]{0:T(1024)}, u32[]{:S(2)}) copy-start(f32[4096]{0:T(1024)} %param.23) | copy-start | bytes 49156
  20.5 64.8 %copy-start.9 = (s32[16,2]{0,1:T(2,128)S(1)}, s32[16,2]{0,1:T(2,128)}, u32[]{:S(2)}) copy-start(s32[16,2]{0,1:T(2,128)} %param.25) | copy-start | bytes 388
  20.5 125.5 %all-gather.6.cloned.1.call-start = ((), (), s32[]{:S(2)}) async-start(), calls=%async_computation.3 | async-start | bytes 4325376 | tf_op jit(solution)/shard_map/all_gather | solution.py:93
  65.5 59.8 %copy-start.10 = (s32[16]{0:T(128)S(1)}, s32[16]{0:T(128)}, u32[]{:S(2)}) copy-start(s32[16]{0:T(128)} %param.31) | copy-start | bytes 196
  65.5 80.5 %copy-start.5 = (bf16[4096,8]{0,1:T(8,128)(2,1)S(1)}, bf16[4096,8]{0,1:T(8,128)(2,1)}, u32[]{:S(2)}) copy-start(bf16[4096,8]{0,1:T(8,128)(2,1)} %param.24) | copy-start | bytes 196612
  146.0 3.9 %copy-start.2 = (bf16[512,4096]{1,0:T(8,128)(2,1)S(1)}, bf16[512,4096]{1,0:T(8,128)(2,1)}, u32[]{:S(2)}) copy-start(bf16[512,4096]{1,0:T(8,128)(2,1)} %all-gather.6.cloned.1.call-done) | copy-start | bytes 12582916
  177.4 23.2 %copy-start.11 = (f32[8]{0:T(128)S(1)}, f32[8]{0:T(128)}, u32[]{:S(2)}) copy-start(f32[8]{0:T(128)} %param.30) | copy-start | bytes 100
  177.4 97.0 %copy-start.7 = (f32[1024]{0:T(1024)S(1)}, f32[1024]{0:T(1024)}, u32[]{:S(2)}) copy-start(f32[1024]{0:T(1024)} %param.29) | copy-start | bytes 12292
  177.4 100.8 %copy-start.1 = (bf16[1024,512]{1,0:T(8,128)(2,1)S(1)}, bf16[1024,512]{1,0:T(8,128)(2,1)}, u32[]{:S(2)}) copy-start(bf16[1024,512]{1,0:T(8,128)(2,1)} %param.22) | copy-start | bytes 3145732
  190.5 9.4 %all-to-all-start.1 = ((f32[4,16,1024]{2,1,0:T(8,128)}), f32[4,16,1024]{2,1,0:T(8,128)S(1)}, u32[]{:S(2)}, u32[]{:S(2)}) async-start(f32[4,16,1024]{2,1,0:T(8,128)} %bitcast.86), calls=%async_computation.1 | async-start | bytes 524288 | tf_op jit(solution)/shard_map/all_to_all | solution.py:137
  193.9 73.9 %all-reduce.2.cloned.1.call-start = ((), (), s32[]{:S(2)}) async-start(), calls=%async_computation.4 | async-start | bytes 131072 | tf_op jit(solution)/shard_map/psum | solution.py:144
  275.4 2.9 %copy-start.8 = (bf16[2,1024]{1,0:T(2,128)(2,1)}, bf16[2,1024]{1,0:T(2,128)(2,1)S(1)}, u32[]{:S(2)}) copy-start(bf16[2,1024]{1,0:T(2,128)(2,1)S(1)} %constant_dynamic-slice_fusion) | copy-start | bytes 12292
Sparse Core Ops, SparseCore 0:
  20.6 42.9 all-gather.3
  85.4 60.5 all-gather.5
  200.7 67.0 all-reduce.1

commit v3 on v2

--- a/solution.py
+++ b/solution.py
@@ -52,6 +52,11 @@
     return context.astype(jnp.bfloat16).reshape(span_count * window, kv_local * group * HD)
 
 
+def spread(block, axes):
+    copies = jnp.broadcast_to(block[None], (lax.axis_size(axes), *block.shape))
+    return lax.all_to_all(copies, axes, split_axis=0, concat_axis=0, tiled=True)
+
+
 def shards(
     residual,
     queries,
@@ -78,13 +83,15 @@
     tokens = tok_local * n_dp * n_ex
     spans = span_local * n_dp
     exact = lax.Precision.HIGHEST
-    all_routes = lax.all_gather(routes, both, axis=0, tiled=True)
     attended = attend(queries, new_keys, new_values, cache_keys, cache_values)
-    rows = lax.all_gather(attended, "dp", axis=0, tiled=True)
+    rows = spread(attended, "dp").reshape(tokens, -1)
     parts = jnp.dot(rows, out_weight, preferred_element_type=jnp.float32).astype(jnp.bfloat16)
-    parts = lax.all_to_all(
-        parts.reshape(n_dp * n_ex, tok_local, -1), both, split_axis=0, concat_axis=0, tiled=True
-    )
+    labels = jnp.pad(routes.astype(jnp.bfloat16), ((0, 0), (0, HD - routes.shape[1])))
+    labels = jnp.broadcast_to(labels[None], (n_dp * n_ex, *labels.shape))
+    parts = jnp.concatenate([parts.reshape(n_dp * n_ex, tok_local, -1), labels], axis=-1)
+    parts = lax.all_to_all(parts, both, split_axis=0, concat_axis=0, tiled=True)
+    all_routes = parts[:, :, -HD : routes.shape[1] - HD].astype(jnp.int32).reshape(tokens, -1)
+    parts = parts[:, :, :-HD]
     terms = jnp.sum(parts.reshape(n_dp, n_ex, tok_local, -1).astype(jnp.float32), axis=1)
     mixed = residual.astype(jnp.float32) + terms.transpose(1, 0, 2).reshape(tok_local, width)
     normed = (
@@ -134,15 +141,14 @@
     token_span = ((dp_index * n_ex + column) * tok_local + jnp.arange(tok_local)) // WIN
     pool_matrix = (token_span[None, :] == jnp.arange(spans)[:, None]).astype(jnp.float32)
     pooled = down[:spans] + down[spans:] + jnp.dot(pool_matrix, mixed, precision=exact)
-    pooled = lax.all_to_all(
-        pooled.reshape(spans, n_ex, -1).transpose(1, 0, 2),
-        "expert",
-        split_axis=0,
-        concat_axis=0,
-        tiled=True,
-    )
-    pooled = lax.psum(jnp.sum(pooled, axis=0), "dp")
-    squares = lax.psum(jnp.sum(pooled * pooled, axis=-1), "expert")
+    pooled = pooled.reshape(n_dp, span_local, n_ex, -1).transpose(0, 2, 1, 3)
+    pooled = pooled.reshape(n_dp * n_ex, span_local, -1)
+    pooled = lax.all_to_all(pooled, both, split_axis=0, concat_axis=0, tiled=True)
+    pooled = jnp.sum(pooled, axis=0)
+    pooled = spread(pooled, both).reshape(n_dp, n_ex, span_local, -1)
+    pooled = pooled.transpose(0, 2, 1, 3).reshape(spans, n_ex, -1)
+    squares = jnp.sum(pooled * pooled, axis=(1, 2))
+    pooled = lax.dynamic_index_in_dim(pooled, column, axis=1, keepdims=False)
     summary = (pooled * lax.rsqrt(squares / width + EPSILON)[:, None] * summary_gain).astype(
         jnp.bfloat16
     )

time: 286 us -> 220 us (0.77)
  waiting for transfers between devices: 136 us -> 95.9 us
  blocking collectives: 63.7 us -> 34.9 us
  starting transfers between devices: 3.53 us -> 9.9 us
  matrix products: 52.5 us -> 49.6 us
    psum x1 -> x0, waiting for transfers between devices: 67.2 us -> none  [shards(): pooled = lax.psum(jnp.sum(pooled, axis=0), 'dp')]
    all_gather x1 -> x0, waiting for transfers between devices: 43 us -> none  [shards(): rows = lax.all_gather(attended, 'dp', axis=0, tiled=True)]
    all_gather x1, waiting for transfers between devices: 20.4 us -> 59.8 us  [shards(): everyone = lax.all_gather(normed, both, axis=0, tiled=True)]
    all_gather x1 -> x0, blocking collectives: 39.3 us -> none  [shards(): all_routes = lax.all_gather(routes, both, axis=0, tiled=True)]
    all_to_all x1 -> x2, waiting for transfers between devices: 5.88 us -> 36 us  [spread(): return lax.all_to_all(copies, axes, split_axis=0, concat_axis=0, tiled=True)]
    all_to_all x1 -> x2, blocking collectives: 18.7 us -> 34.9 us  [the longest x1 21.3 us: shards(): parts = lax.all_to_all(parts, both, split_axis=0, concat_axis=0, tiled=True)]
    all_to_all x1 -> x2, starting transfers between devices: 3.4 us -> 9.86 us  [spread(): return lax.all_to_all(copies, axes, split_axis=0, concat_axis=0, tiled=True)]
    psum x1 -> x0, blocking collectives: 5.66 us -> none  [shards(): squares = lax.psum(jnp.sum(pooled * pooled, axis=-1), 'expert')]
  transfers between devices with their start and end apart: 4 -> 3, of which waited for: 4 -> 3; matrix products, arithmetic and copies ran while one was open for 0% -> 1% of each run, Pallas kernels for 0% -> 0%
where the time goes in v3:
time: 220 us; the launch traced here: 219 us
  waiting for transfers between devices  95.9 us (44%)
  matrix products  49.6 us (23%)
  blocking collectives  34.9 us (16%)
  between operations  14.4 us (7%)
  local copies, waits for them, and re-layouts  11.7 us (5%)
  starting transfers between devices  9.9 us (4%)
  other arithmetic  3.06 us (1%)
    all_gather x1, waiting for transfers between devices, shards(): everyone = lax.all_gather(normed, both, axis=0, tiled=True)  59.8 us
    all_to_all x2, waiting for transfers between devices, spread(): return lax.all_to_all(copies, axes, split_axis=0, concat_axis=0, tiled=True)  36 us
    all_to_all x1, blocking collectives, shards(): parts = lax.all_to_all(parts, both, split_axis=0, concat_axis=0, tiled=True)  21.3 us
    all_to_all x1, blocking collectives, shards(): lax.all_to_all(pooled, both, split_axis=0, concat_axis=0, tiled=True)  13.6 us
    dot_general x1, matrix products, shards(): jnp.einsum('end,edf->enf', compact, w_up, preferred_element_type=jnp.floa...  12.5 us
    dot_general x1, matrix products, shards(): jnp.einsum('end,edf->enf', compact, w_gate, preferred_element_type=jnp.fl...  12.4 us
    dot_general x1, matrix products, shards(): jnp.dot(halves, w_down.reshape(-1, width), preferred_element_type=jnp.flo...  12.1 us
    all_to_all x2, starting transfers between devices, spread(): return lax.all_to_all(copies, axes, split_axis=0, concat_axis=0, tiled=True)  9.86 us
  transfers between devices with their start and end apart: 3, of which 3 were waited for; matrix products, arithmetic and copies ran while one was open for 1% of the time, Pallas kernels for 0%

profile of v3, /device:TPU:0, one launch (start us, length us, event | category | flops | bytes accessed | tf_op | source)
XLA Modules:
  0.0 219.4 jit_solution(10095825210046443135)
XLA Ops:
  7.2 0.0 copy-start
  7.2 1.5 reshape.317
  8.7 1.4 reshape.319
  10.0 1.0 reshape.316
  11.0 2.2 reshape.315
  13.2 1.8 bitcast_reduce_fusion
  14.9 0.3 fusion.47
  15.3 0.1 fusion.17
  15.4 0.5 fusion.2
  15.9 2.2 reshape.318
  18.0 1.9 fusion.11
  20.0 0.0 copy-start.10
  20.0 0.3 fusion.6
  20.3 0.1 copy.111
  20.3 0.1 broadcast_in_dim.83
  20.4 1.1 broadcast_in_dim.84
  21.5 7.3 %all-to-all-start = ((bf16[8,64,1024]{2,1,0:T(8,128)(2,1)}), bf16[8,64,1024]{2,1,0:T(8,128)(2,1)S(1)}, u32[]{:S(2)}, u32[]{:S(2)}) async-start(bf16[8,64,1024]{2,1,0:T(8,128)(2,1)} %broadcast_in_dim.84), calls=%async_computation | async-start | bytes 2097152 | tf_op jit(solution)/shard_map/all_to_all | solution.py:57
  28.8 0.0 all-gather.2.cloned.1.call-start
  28.9 0.1 copy.138
  29.0 25.6 %all-to-all-done = bf16[8,64,1024]{2,1,0:T(8,128)(2,1)S(1)} async-done(((bf16[8,64,1024]{2,1,0:T(8,128)(2,1)}), bf16[8,64,1024]{2,1,0:T(8,128)(2,1)S(1)}, u32[]{:S(2)}, u32[]{:S(2)}) %all-to-all-start) | async-done | bytes 1048608 | tf_op jit(solution)/shard_map/all_to_all | solution.py:57
  54.6 0.7 convolution_convert_fusion.1
  55.4 0.1 pad_maximum_fusion
  55.4 21.3 %all_to_all.20 = bf16[32,16,640]{2,1,0:T(8,128)(2,1)S(1)} all-to-all(bf16[32,16,640]{2,1,0:T(8,128)(2,1)S(1)} %pad_maximum_fusion), channel_id=1, replica_groups=mesh['dp'=8,'expert'=4] {'dp','expert'}, dimensions={0} | all-to-all | bytes 1310720 | tf_op jit(solution)/shard_map/all_to_all | solution.py:92
  76.8 0.1 convert_reduce_fusion
  76.9 0.2 multiply_reduce_fusion.1
  77.0 0.7 multiply_convert_fusion.1
  77.8 0.0 all-gather.2.cloned.1.call-update
  77.8 0.1 eq.145
  78.0 0.2 copy.137
  78.2 0.1 copy.114
  78.3 0.1 reshape.334
  78.4 0.1 compare_or_fusion
  78.4 0.2 convolution_convert_fusion.3
  78.6 0.2 fusion.16
  78.8 0.2 select_reduce_fusion.1
  79.1 59.8 %all-gather.2.cloned.1.call-done = bf16[512,4096]{1,0:T(8,128)(2,1)} async-done(((bf16[16,4096]{1,0:T(8,128)(2,1)}), bf16[512,4096]{1,0:T(8,128)(2,1)}) %all-gather.2.cloned.1.call-update) | async-done | bytes 4194320 | tf_op jit(solution)/shard_map/all_gather | solution.py:100
  138.9 3.5 %select_reduce_fusion.3 = (f32[512]{0:T(512)S(1)}, f32[512]{0:T(512)S(1)}) fusion(s32[512]{0:T(512)S(1)} %bitcast.98, s32[512]{0:T(512)S(1)} %bitcast.101, bf16[512,4096]{1,0:T(8,128)(2,1)} %all-gather.2.cloned.1.call-done, bf16[4096,8]{0,1:T(8,128)(2,1)S(1)} %copy-done.5), kind=kOutput, calls=%fused_computation.68 | convolution fusion | flops 33577984 | bytes 4268032 | tf_op jit(solution)/shard_map/dot_general | solution.py:119
  142.5 0.1 compare_select_fusion.1
  142.5 0.2 select_reduce_fusion
  142.8 1.8 convolution_convert_fusion
  144.6 12.4 %fusion.53 = f32[2,192,1792]{2,1,0:T(8,128)S(1)} fusion(bf16[2,192,4096]{2,1,0:T(8,128)(2,1)S(1)} %bitcast.80, bf16[2,4096,1792]{2,1,0:T(8,128)(2,1)} %param.26), kind=kOutput, calls=%fused_computation.108 | convolution fusion | flops 5637144576 | bytes 35258368 | tf_op jit(solution)/shard_map/end,edf->enf/dot_general | solution.py:133
  157.0 12.5 %multiply_convert_fusion = bf16[2,192,1792]{2,1,0:T(8,128)(2,1)S(1)} fusion(f32[2,192,1792]{2,1,0:T(8,128)S(1)} %fusion.53, bf16[2,192,4096]{2,1,0:T(8,128)(2,1)S(1)} %bitcast.81, bf16[2,4096,1792]{2,1,0:T(8,128)(2,1)} %param.27), kind=kOutput, calls=%fused_computation.3 | convolution fusion | flops 5641273344 | bytes 36634624 | tf_op jit(solution)/shard_map/end,edf->enf/dot_general | solution.py:134
  169.6 0.6 convolution_bitcast_fusion
  170.3 12.1 %fusion.19 = f32[32,4096]{1,0:T(8,128)S(1)} fusion(bf16[3584,4096]{1,0:T(8,128)(2,1)} %bitcast.79, bf16[16,3584]{1,0:T(8,128)(2,1)S(1)} %get-tuple-element.5, bf16[16,3584]{1,0:T(8,128)(2,1)S(1)} %get-tuple-element.4), kind=kOutput, calls=%fused_computation.48 | convolution fusion | flops 939982848 | bytes 30113792 | tf_op jit(solution)/shard_map/dot_general | solution.py:140
  182.4 0.0 copy-start.11
  182.4 0.3 convolution_add_fusion
  182.7 0.2 reshape.328
  182.9 0.2 copy.118
  183.1 13.6 %all_to_all.21 = f32[32,2,1024]{2,1,0:T(2,128)S(1)} all-to-all(f32[32,2,1024]{2,1,0:T(2,128)S(1)} %bitcast.91), channel_id=1, replica_groups=mesh['dp'=8,'expert'=4] {'dp','expert'}, dimensions={0} | all-to-all | bytes 524288 | tf_op jit(solution)/shard_map/all_to_all | solution.py:146
  196.6 0.1 reduce_sum.107
  196.7 0.8 broadcast_in_dim.143
  197.5 2.6 %all-to-all-start.3 = ((f32[32,2,1024]{2,1,0:T(2,128)}), f32[32,2,1024]{2,1,0:T(2,128)S(1)}, u32[]{:S(2)}, u32[]{:S(2)}) async-start(f32[32,2,1024]{2,1,0:T(2,128)} %broadcast_in_dim.143), calls=%async_computation.3 | async-start | bytes 524288 | tf_op jit(solution)/shard_map/all_to_all | solution.py:57
  200.1 0.1 dynamic_slice.12
  200.2 0.1 broadcast_compare_fusion
  200.3 10.4 %all-to-all-done.3 = f32[32,2,1024]{2,1,0:T(2,128)S(1)} async-done(((f32[32,2,1024]{2,1,0:T(2,128)}), f32[32,2,1024]{2,1,0:T(2,128)S(1)}, u32[]{:S(2)}, u32[]{:S(2)}) %all-to-all-start.3) | async-done | bytes 262176 | tf_op jit(solution)/shard_map/all_to_all | solution.py:57
  210.7 0.2 multiply_reduce_fusion
  210.9 0.1 copy.119
  211.0 0.1 rsqrt.20
  211.1 0.1 dynamic-slice
  211.2 0.1 constant_dynamic-slice_fusion
  211.3 0.1 multiply_convert_fusion.2
  211.4 0.1 fusion.36
  211.4 0.3 fusion.48
  211.7 0.8 fusion.10
  (44 shorter events, 0.3 us)
Async XLA Ops:
  7.2 47.4 %copy-start = (bf16[1024,512]{1,0:T(8,128)(2,1)S(1)}, bf16[1024,512]{1,0:T(8,128)(2,1)}, u32[]{:S(2)}) copy-start(bf16[1024,512]{1,0:T(8,128)(2,1)} %param.22) | copy-start | bytes 3145732
  13.2 1.8 copy-start.4
  18.0 2.0 copy-start.6
  20.0 8.9 %copy-start.10 = (s32[16,2]{0,1:T(2,128)S(1)}, s32[16,2]{0,1:T(2,128)}, u32[]{:S(2)}) copy-start(s32[16,2]{0,1:T(2,128)} %param.25) | copy-start | bytes 388
  21.5 33.1 %all-to-all-start = ((bf16[8,64,1024]{2,1,0:T(8,128)(2,1)}), bf16[8,64,1024]{2,1,0:T(8,128)(2,1)S(1)}, u32[]{:S(2)}, u32[]{:S(2)}) async-start(bf16[8,64,1024]{2,1,0:T(8,128)(2,1)} %broadcast_in_dim.84), calls=%async_computation | async-start | bytes 2097152 | tf_op jit(solution)/shard_map/all_to_all | solution.py:57
  28.8 110.1 %all-gather.2.cloned.1.call-start = ((), (), s32[]{:S(2)}) async-start(), calls=%async_computation.4 | async-start | bytes 4325376 | tf_op jit(solution)/shard_map/all_gather | solution.py:100
  55.3 21.5 %copy-start.3 = (bf16[16,4096]{1,0:T(8,128)(2,1)S(1)}, bf16[16,4096]{1,0:T(8,128)(2,1)}, u32[]{:S(2)}) copy-start(bf16[16,4096]{1,0:T(8,128)(2,1)} %param.16) | copy-start | bytes 393220
  55.3 21.7 %copy-start.7 = (f32[4096]{0:T(1024)S(1)}, f32[4096]{0:T(1024)}, u32[]{:S(2)}) copy-start(f32[4096]{0:T(1024)} %param.23) | copy-start | bytes 49156
  55.4 83.5 %copy-start.5 = (bf16[4096,8]{0,1:T(8,128)(2,1)S(1)}, bf16[4096,8]{0,1:T(8,128)(2,1)}, u32[]{:S(2)}) copy-start(bf16[4096,8]{0,1:T(8,128)(2,1)} %param.24) | copy-start | bytes 196612
  138.9 3.9 %copy-start.2 = (bf16[512,4096]{1,0:T(8,128)(2,1)S(1)}, bf16[512,4096]{1,0:T(8,128)(2,1)}, u32[]{:S(2)}) copy-start(bf16[512,4096]{1,0:T(8,128)(2,1)} %all-gather.2.cloned.1.call-done) | copy-start | bytes 12582916
  170.3 42.3 %copy-start.1 = (bf16[1024,512]{1,0:T(8,128)(2,1)S(1)}, bf16[1024,512]{1,0:T(8,128)(2,1)}, u32[]{:S(2)}) copy-start(bf16[1024,512]{1,0:T(8,128)(2,1)} %param.22) | copy-start | bytes 3145732
  182.4 17.7 %copy-start.12 = (s32[16]{0:T(128)S(1)}, s32[16]{0:T(128)}, u32[]{:S(2)}) copy-start(s32[16]{0:T(128)} %param.31) | copy-start | bytes 196
  182.4 17.8 %copy-start.11 = (f32[8]{0:T(128)S(1)}, f32[8]{0:T(128)}, u32[]{:S(2)}) copy-start(f32[8]{0:T(128)} %param.30) | copy-start | bytes 100
  182.4 28.9 %copy-start.8 = (f32[1024]{0:T(1024)S(1)}, f32[1024]{0:T(1024)}, u32[]{:S(2)}) copy-start(f32[1024]{0:T(1024)} %param.29) | copy-start | bytes 12292
  197.5 13.2 %all-to-all-start.3 = ((f32[32,2,1024]{2,1,0:T(2,128)}), f32[32,2,1024]{2,1,0:T(2,128)S(1)}, u32[]{:S(2)}, u32[]{:S(2)}) async-start(f32[32,2,1024]{2,1,0:T(2,128)} %broadcast_in_dim.143), calls=%async_computation.3 | async-start | bytes 524288 | tf_op jit(solution)/shard_map/all_to_all | solution.py:57
  211.4 1.1 copy-start.9
Sparse Core Ops, SparseCore 0:
  77.9 60.9 all-gather.1
